TPU v7x, 32 devices: a whole 2x2x4 slice. The times are simulated.
32 devices in a mesh: dp: 8 (over z, x), mp: 4 (over y, core).
Axes of the slice: x: 2, y: 2, z: 4, core: 2. Of those that a mesh axis runs over, the one named last changes fastest.
Arguments:
- images: bfloat16 [800, 198, 384], P(('dp', 'mp')), may hold values from -6 to 6
- keep_mask: int32 [800, 198], P(('dp', 'mp')), may hold values from 0 to 1, as said below
- kept_counts: int32 [800], P(('dp', 'mp')), may hold values from 20 to 198, as said below
- pack_offsets: int32 [800], P(('dp', 'mp')), may hold values from 0 to 2027, as said below
- segment_ids: int32 [65536], P(('dp', 'mp')), may hold values from 0 to 25, as said below
- cotangent: bfloat16 [65536, 384], P(('dp', 'mp')), may hold values from -6 to 6
- attn_weight: float32 [384, 1536], P(None, ('dp', 'mp'))
- ffn_weight: float32 [2, 384, 1536], P(None, None, ('dp', 'mp'))
- up_bias: float32 [1536], P(('dp', 'mp')), may hold values from -3 to 3
- vectors: float32 [8, 384], replicated
- attn_first: float32 [384, 1536], P(None, ('dp', 'mp')), may hold values from -80 to 80
- ffn_first: float32 [2, 384, 1536], P(None, None, ('dp', 'mp')), may hold values from -64 to 64
- bias_first: float32 [1536], P(('dp', 'mp')), may hold values from -48 to 48
- vec_first: float32 [8, 384], replicated, may hold values from -160 to 160
- attn_second: float32 [384, 1536], P(None, ('dp', 'mp')), may hold values from 8.192 to 131.072
- ffn_second: float32 [2, 384, 1536], P(None, None, ('dp', 'mp')), may hold values from 5.24288 to 83.88608
- bias_second: float32 [1536], P(('dp', 'mp')), may hold values from 2.94912 to 47.18592
- vec_second: float32 [8, 384], replicated, may hold values from 32.768 to 524.288
- attn_average: float32 [384, 1536], P(None, ('dp', 'mp')), may hold values from -0.3125 to 0.3125
- ffn_average: float32 [2, 384, 1536], P(None, None, ('dp', 'mp')), may hold values from -0.3125 to 0.3125
- bias_average: float32 [1536], P(('dp', 'mp')), may hold values from -3 to 3
- vec_average: float32 [8, 384], replicated, may hold values from -0.5 to 1.5
- step: int32 [1], replicated, may hold values from 1 to 20
Outputs:
- layer_out: bfloat16 [65536, 384], P(('dp', 'mp'))
- image_grads: float32 [800, 198, 384], P(('dp', 'mp'))
- attn_grad: float32 [384, 1536], P(None, ('dp', 'mp'))
- ffn_grad: float32 [2, 384, 1536], P(None, None, ('dp', 'mp'))
- bias_grad: float32 [1536], P(('dp', 'mp'))
- vec_grad: float32 [8, 384], replicated
- attn_new: float32 [384, 1536], P(None, ('dp', 'mp'))
- ffn_new: float32 [2, 384, 1536], P(None, None, ('dp', 'mp'))
- bias_new: float32 [1536], P(('dp', 'mp'))
- vec_new: float32 [8, 384], replicated
- attn_first_new: float32 [384, 1536], P(None, ('dp', 'mp'))
- ffn_first_new: float32 [2, 384, 1536], P(None, None, ('dp', 'mp'))
- bias_first_new: float32 [1536], P(('dp', 'mp'))
- vec_first_new: float32 [8, 384], replicated
- attn_second_new: float32 [384, 1536], P(None, ('dp', 'mp'))
- ffn_second_new: float32 [2, 384, 1536], P(None, None, ('dp', 'mp'))
- bias_second_new: float32 [1536], P(('dp', 'mp'))
- vec_second_new: float32 [8, 384], replicated
- attn_average_new: float32 [384, 1536], P(None, ('dp', 'mp'))
- ffn_average_new: float32 [2, 384, 1536], P(None, None, ('dp', 'mp'))
- bias_average_new: float32 [1536], P(('dp', 'mp'))
- vec_average_new: float32 [8, 384], replicated
Inputs may be any that keep to these rules, and one draw needn't show every extreme that they name: `keep_mask`: each image keeps exactly kept_counts of its tokens, its first two among them. `kept_counts`: on every device the last image keeps 20 tokens and one of the others keeps all 198; the counts of a device's 25 images sum to 2047. `pack_offsets`: A device's images fill its pack in order from row 0 without gaps: an image's offset is the sum of the kept counts of the device's earlier images. `segment_ids`: each pack row carries the number of the image that fills it; 25 marks the last row of every pack, which is unused.
All inputs are finite; a program needn't handle non-finite values.
Results may differ from a plain program's by a relative error of at most 0.01.
The roundings to bfloat16 on the way count: a program that leaves them out, or rounds other values in their place, can miss the bound.
Values may be sent and summed in bfloat16 or wider, within the bound.
No kernel may reach another device: no remote copies, remote signals or barrier semaphores. Data moves between devices by JAX's collectives and lax.ppermute only.
A program may use at most 320 MiB of HBM per device.

v0:
```python
import math

import jax
import jax.numpy as jnp
from jax import lax
from jax.sharding import PartitionSpec as P

HEADS = 6
HEAD = 64


NORM_EPS = 1e-06
BETA_ONE = 0.9
BETA_TWO = 0.999
ADAM_EPS = 1e-08
MATRIX_RATE = 0.05
VECTOR_RATE = 0.2
WEIGHT_DECAY = 0.05
AVERAGE_DECAY = 0.8


def layer_norm(values, gain, shift):
    centre = jnp.mean(values, axis=-1, keepdims=True)
    centred = values - centre
    spread = jnp.mean(centred * centred, axis=-1, keepdims=True)
    return centred * lax.rsqrt(spread + NORM_EPS) * gain + shift


def pack_rows(keep_mask, kept_counts, pack_offsets, segment_ids):
    images_here = keep_mask.shape[0]
    length = keep_mask.shape[1]
    ranks = jnp.cumsum(keep_mask, axis=1) - 1
    slots = jnp.where(keep_mask > 0, ranks, length)
    image_row = jnp.broadcast_to(jnp.arange(images_here, dtype=jnp.int32)[:, None], keep_mask.shape)
    token_col = jnp.broadcast_to(jnp.arange(length, dtype=jnp.int32)[None, :], keep_mask.shape)
    position = jnp.zeros((images_here, length + 1), jnp.int32).at[image_row, slots].set(token_col)
    owner = jnp.minimum(segment_ids, images_here - 1)
    local = jnp.arange(segment_ids.shape[0], dtype=jnp.int32) - pack_offsets[owner]
    valid = (segment_ids < images_here) & (local >= 0) & (local < kept_counts[owner])
    local = jnp.clip(local, 0, length - 1)
    source = owner * length + position[owner, local]
    return (source, valid)


def gelu_exact(values):
    return jax.nn.gelu(values, approximate=False)


def adamw(weight, grad, first, second, average, count, rate, decay):
    first_new = BETA_ONE * first + (1.0 - BETA_ONE) * grad
    second_new = BETA_TWO * second + (1.0 - BETA_TWO) * grad * grad
    first_hat = first_new / (1.0 - jnp.power(BETA_ONE, count))
    second_hat = second_new / (1.0 - jnp.power(BETA_TWO, count))
    weight_new = weight - rate * (first_hat / (jnp.sqrt(second_hat) + ADAM_EPS) + decay * weight)
    average_new = AVERAGE_DECAY * average + (1.0 - AVERAGE_DECAY) * weight_new
    return (weight_new, first_new, second_new, average_new)


def contract_rows(left, right):
    return lax.dot_general(
        left, right, (((0,), (0,)), ((), ())), preferred_element_type=jnp.float32
    )


def contract_cols(left, right):
    return lax.dot_general(
        left, right, (((1,), (1,)), ((), ())), preferred_element_type=jnp.float32
    )


def body(
    images,
    keep_mask,
    kept_counts,
    pack_offsets,
    segment_ids,
    cotangent,
    attn_weight,
    ffn_weight,
    up_bias,
    vectors,
    attn_first,
    ffn_first,
    bias_first,
    vec_first,
    attn_second,
    ffn_second,
    bias_second,
    vec_second,
    attn_average,
    ffn_average,
    bias_average,
    vec_average,
    step,
):
    width = images.shape[2]
    rows = segment_ids.shape[0]
    scale = 1.0 / math.sqrt(HEAD)
    attn_full = lax.all_gather(attn_weight.astype(jnp.bfloat16), ("dp", "mp"), axis=1, tiled=True)
    ffn_full, bias_full = (
        lax.all_gather(ffn_weight.astype(jnp.bfloat16), "dp", axis=2, tiled=True),
        lax.all_gather(up_bias.astype(jnp.bfloat16), "dp", axis=0, tiled=True),
    )
    w_qkv = attn_full[:, : 3 * width]
    w_out = attn_full[:, 3 * width :]
    w_up = ffn_full[0]
    w_down = ffn_full[1]
    up_shift = bias_full.astype(jnp.float32)
    source, valid = pack_rows(keep_mask, kept_counts, pack_offsets, segment_ids)
    inputs = jnp.where(valid[:, None], images.reshape(-1, width)[source].astype(jnp.float32), 0.0)
    normed_f, norm_one_back = jax.vjp(layer_norm, inputs, vectors[0], vectors[1])
    normed = normed_f.astype(jnp.bfloat16)
    qkv_bias = jnp.concatenate([vectors[2], jnp.zeros_like(vectors[2]), vectors[3]])
    qkv = (jnp.dot(normed, w_qkv, preferred_element_type=jnp.float32) + qkv_bias).astype(
        jnp.bfloat16
    )
    query = qkv[:, :width].reshape(rows, HEADS, HEAD)
    key_rows = qkv[:, width : 2 * width].reshape(rows, HEADS, HEAD)
    value = qkv[:, 2 * width :].reshape(rows, HEADS, HEAD)
    block = min(512, rows)
    starts = list(range(0, rows, block))

    def block_scores(lower):
        raw = jnp.einsum(
            "qhd,khd->hqk",
            query[lower : lower + block],
            key_rows,
            preferred_element_type=jnp.float32,
        )
        same = segment_ids[lower : lower + block, None] == segment_ids[None, :]
        return (jnp.where(same[None], raw * scale, -1000000000.0), same)

    mixed_parts = []
    lse_parts = []
    for lower in starts:
        scores, same = block_scores(lower)
        top = jnp.max(scores, axis=-1, keepdims=True)
        expo = jnp.exp(scores - top)
        total = jnp.sum(expo, axis=-1, keepdims=True)
        probs_low = (expo / total).astype(jnp.bfloat16)
        mixed_parts.append(
            jnp.einsum("hqk,khd->qhd", probs_low, value, preferred_element_type=jnp.float32)
        )
        lse_parts.append(top + jnp.log(total))
    mixed = jnp.concatenate(mixed_parts, axis=0).reshape(rows, width).astype(jnp.bfloat16)
    middle = inputs + jnp.dot(mixed, w_out, preferred_element_type=jnp.float32) + vectors[4]
    normed_two_f, norm_two_back = jax.vjp(layer_norm, middle, vectors[5], vectors[6])
    normed_two = normed_two_f.astype(jnp.bfloat16)
    gathered = lax.all_gather(normed_two, "mp", axis=0, tiled=True)
    hidden_in = jnp.dot(gathered, w_up, preferred_element_type=jnp.float32) + up_shift
    hidden = gelu_exact(hidden_in).astype(jnp.bfloat16)
    down = lax.psum_scatter(contract_cols(hidden, w_down), "mp", scatter_dimension=0, tiled=True)
    layer_out = jnp.where(valid[:, None], middle + down + vectors[7], 0.0).astype(jnp.bfloat16)
    grad_out = jnp.where(valid[:, None], cotangent.astype(jnp.float32), 0.0)
    grad_low = grad_out.astype(jnp.bfloat16)
    down_bias_grad = jnp.sum(grad_out, axis=0)
    piece = lax.all_gather(grad_low, "mp", axis=0, tiled=True)
    grad_rows = jnp.dot(piece, w_down, preferred_element_type=jnp.float32)
    grad_in_rows = jax.vjp(gelu_exact, hidden_in)[1](grad_rows)[0]
    down_total = contract_rows(piece, hidden)
    bias_total = jnp.sum(grad_in_rows, axis=0)
    grads_in = grad_in_rows.astype(jnp.bfloat16)
    normed_two_grad = lax.psum_scatter(
        contract_cols(grads_in, w_up), "mp", scatter_dimension=0, tiled=True
    )
    up_grad = contract_rows(gathered, grads_in)
    middle_norm_grad, gain_two_grad, shift_two_grad = norm_two_back(normed_two_grad)
    middle_grad = grad_out + middle_norm_grad
    out_bias_grad = jnp.sum(middle_grad, axis=0)
    middle_low = middle_grad.astype(jnp.bfloat16)
    out_grad = contract_rows(mixed, middle_low)
    mixed_grad = contract_cols(middle_low, w_out).astype(jnp.bfloat16).reshape(rows, HEADS, HEAD)
    query_parts = []
    key_grad = jnp.zeros((rows, HEADS, HEAD), jnp.float32)
    value_grad = jnp.zeros((rows, HEADS, HEAD), jnp.float32)
    for index, lower in enumerate(starts):
        scores, same = block_scores(lower)
        probs = jnp.exp(scores - lse_parts[index])
        part_grad = mixed_grad[lower : lower + block]
        prob_grad = jnp.einsum("qhd,khd->hqk", part_grad, value, preferred_element_type=jnp.float32)
        inner = jnp.sum(probs * prob_grad, axis=-1, keepdims=True)
        score_grad = jnp.where(same[None], probs * (prob_grad - inner) * scale, 0.0).astype(
            jnp.bfloat16
        )
        query_parts.append(
            jnp.einsum("hqk,khd->qhd", score_grad, key_rows, preferred_element_type=jnp.float32)
        )
        key_grad = key_grad + jnp.einsum(
            "hqk,qhd->khd",
            score_grad,
            query[lower : lower + block],
            preferred_element_type=jnp.float32,
        )
        value_grad = value_grad + jnp.einsum(
            "hqk,qhd->khd",
            probs.astype(jnp.bfloat16),
            part_grad,
            preferred_element_type=jnp.float32,
        )
    qkv_grad = jnp.concatenate(
        [
            jnp.concatenate(query_parts, axis=0).reshape(rows, width),
            key_grad.reshape(rows, width),
            value_grad.reshape(rows, width),
        ],
        axis=1,
    ).astype(jnp.bfloat16)
    qkv_bias_grad = jnp.sum(qkv_grad, axis=0, dtype=jnp.float32)
    qkv_weight_grad = contract_rows(normed, qkv_grad)
    normed_grad = contract_cols(qkv_grad, w_qkv)
    input_norm_grad, gain_one_grad, shift_one_grad = norm_one_back(normed_grad)
    input_grad = middle_grad + input_norm_grad
    image_grads = (
        jnp.zeros((images.shape[0] * images.shape[1], width), jnp.float32)
        .at[source]
        .add(jnp.where(valid[:, None], input_grad, 0.0))
        .reshape(images.shape)
    )
    attn_terms = jnp.concatenate([qkv_weight_grad, out_grad], axis=1)
    ffn_terms = jnp.stack([up_grad, down_total])
    vec_terms = jnp.stack(
        [
            gain_one_grad,
            shift_one_grad,
            qkv_bias_grad[:width],
            qkv_bias_grad[2 * width :],
            out_bias_grad,
            gain_two_grad,
            shift_two_grad,
            down_bias_grad,
        ]
    )
    attn_grad = lax.psum_scatter(attn_terms, ("dp", "mp"), scatter_dimension=1, tiled=True)
    ffn_grad, bias_grad = (
        lax.psum_scatter(ffn_terms, "dp", scatter_dimension=2, tiled=True),
        lax.psum_scatter(bias_total, "dp", scatter_dimension=0, tiled=True),
    )
    vec_grad = lax.psum(vec_terms, ("dp", "mp"))
    count = step[0].astype(jnp.float32)
    attn_up = adamw(
        attn_weight,
        attn_grad,
        attn_first,
        attn_second,
        attn_average,
        count,
        MATRIX_RATE,
        WEIGHT_DECAY,
    )
    ffn_up = adamw(
        ffn_weight, ffn_grad, ffn_first, ffn_second, ffn_average, count, MATRIX_RATE, WEIGHT_DECAY
    )
    bias_up = adamw(
        up_bias, bias_grad, bias_first, bias_second, bias_average, count, VECTOR_RATE, 0.0
    )
    vec_up = adamw(vectors, vec_grad, vec_first, vec_second, vec_average, count, VECTOR_RATE, 0.0)
    return (
        layer_out,
        image_grads,
        attn_grad,
        ffn_grad,
        bias_grad,
        vec_grad,
        attn_up[0],
        ffn_up[0],
        bias_up[0],
        vec_up[0],
        attn_up[1],
        ffn_up[1],
        bias_up[1],
        vec_up[1],
        attn_up[2],
        ffn_up[2],
        bias_up[2],
        vec_up[2],
        attn_up[3],
        ffn_up[3],
        bias_up[3],
        vec_up[3],
    )


def solution(mesh):
    placed = (
        P(("dp", "mp"), None, None),
        P(("dp", "mp"), None),
        P(("dp", "mp")),
        P(("dp", "mp")),
        P(("dp", "mp")),
        P(("dp", "mp"), None),
        P(None, ("dp", "mp")),
        P(None, None, ("dp", "mp")),
        P(("dp", "mp")),
        P(),
        P(None, ("dp", "mp")),
        P(None, None, ("dp", "mp")),
        P(("dp", "mp")),
        P(),
        P(None, ("dp", "mp")),
        P(None, None, ("dp", "mp")),
        P(("dp", "mp")),
        P(),
        P(None, ("dp", "mp")),
        P(None, None, ("dp", "mp")),
        P(("dp", "mp")),
        P(),
        P(),
    )
    return jax.shard_map(
        body,
        mesh=mesh,
        in_specs=placed,
        out_specs=(
            P(("dp", "mp"), None),
            P(("dp", "mp"), None, None),
            P(None, ("dp", "mp")),
            P(None, None, ("dp", "mp")),
            P(("dp", "mp")),
            P(),
            P(None, ("dp", "mp")),
            P(None, None, ("dp", "mp")),
            P(("dp", "mp")),
            P(),
            P(None, ("dp", "mp")),
            P(None, None, ("dp", "mp")),
            P(("dp", "mp")),
            P(),
            P(None, ("dp", "mp")),
            P(None, None, ("dp", "mp")),
            P(("dp", "mp")),
            P(),
            P(None, ("dp", "mp")),
            P(None, None, ("dp", "mp")),
            P(("dp", "mp")),
            P(),
        ),
        check_vma=False,
    )
```

profile of v0, /device:TPU:0, one launch (start us, length us, event | category | flops | bytes accessed | tf_op | source)
XLA Modules:
  0.0 1265.6 jit_solution(6935783849205501271)
XLA Ops:
  22.6 24.4 %scatter_custom_fusion.1 = s32[4975]{0:T(1024)S(1)} fusion(s32[4950]{0:T(1024)S(1)} %reshape.454, s32[4950]{0:T(1024)S(1)} %reshape.456, s32[]{:T(128)} %constant.58.clone.1), kind=kCustom, calls=%fused_computation.187 | custom fusion | bytes 19904
  47.1 16.7 %select_select_fusion = s32[2048]{0:T(1024)S(1)} fusion(s32[]{:T(128)} %bitcast, s32[]{:T(128)} %bitcast.1, s32[]{:T(128)} %bitcast.2, s32[]{:T(128)} %bitcast.3, s32[]{:T(128)} %bitcast.4, s32[]{:T(128)} %bitcast.5, s32[]{:T(128)} %bitcast.6, s32[]{:T(128)} %bitcast.7, s32[]{:T(128)} %bitcast.8, s32[]{:T(128)} %bitcast.9, s32[]{:T(128)} %bitcast.10, ...), kind=kLoop, calls=%fused_computation.195 | loop fusion | flops 106496 | bytes 16484 | tf_op jit(solution)/shard_map/gather | solution.py:38
  63.9 16.6 %gather_fusion = s32[2048]{0:T(1024)S(1)} fusion(s32[25,199]{1,0:T(8,128)S(1)} %reshape.367, s32[2048]{0:T(1024)S(1)} %bitcast.160), kind=kCustom, calls=%fused_computation | custom fusion | bytes 32768 | tf_op jit(solution)/shard_map/gather | solution.py:41
  103.6 31.3 %and_and_fusion = pred[2048]{0:T(1024)(128)(4,1)S(1)} fusion(s32[2048]{0:T(1024)S(1)} %copy-done.42, s32[]{:T(128)} %bitcast.25, s32[]{:T(128)} %bitcast.26, s32[]{:T(128)} %bitcast.27, s32[]{:T(128)} %bitcast.28, s32[]{:T(128)} %bitcast.29, s32[]{:T(128)} %bitcast.30, s32[]{:T(128)} %bitcast.31, s32[]{:T(128)} %bitcast.32, s32[]{:T(128)} %bitcast.33, ...), kind=kLoop, calls=%fused_computation.203 | loop fusion | flops 167936 | bytes 10440 | tf_op jit(solution)/shard_map/and | solution.py:39
  168.5 20.7 %fusion.10 = (f32[6,512]{1,0:T(8,128)S(1)}, f32[6,512]{1,0:T(8,128)S(1)}) fusion(f32[6,512,2048]{2,1,0:T(8,128)} %get-tuple-element.227, f32[6,512]{1,0:T(8,128)S(1)} %get-tuple-element.226, pred[512,2048]{1,0:T(8,128)(4,1)S(1)} %copy-done.15, f32[6,512]{1,0:T(8,128)S(1)} %get-tuple-element.224, f32[6,512,2048]{2,1,0:T(8,128)} %get-tuple-element.225, ...), kind=kLoop, calls=%fused_computation.38 | loop fusion | flops 50325504 | bytes 52477952 | tf_op jit(solution)/shard_map/reduce_sum | solution.py:139
  234.2 20.7 %fusion.8 = (f32[6,512]{1,0:T(8,128)S(1)}, f32[6,512]{1,0:T(8,128)S(1)}) fusion(f32[6,512,2048]{2,1,0:T(8,128)} %get-tuple-element.231, f32[6,512]{1,0:T(8,128)S(1)} %get-tuple-element.230, pred[512,2048]{1,0:T(8,128)(4,1)S(1)} %get-tuple-element.164, f32[6,512]{1,0:T(8,128)S(1)} %get-tuple-element.228, f32[6,512,2048]{2,1,0:T(8,128)} %get-tuple-element.229, ...), kind=kLoop, calls=%fused_computation.36 | loop fusion | flops 50325504 | bytes 52477952 | tf_op jit(solution)/shard_map/reduce_sum | solution.py:139
  286.8 23.1 %all-reduce.1 = bf16[384]{0:T(512)(128)(2,1)S(1)} all-reduce(bf16[384]{0:T(512)(128)(2,1)S(1)} %dynamic-update-slice), channel_id=1, replica_groups=mesh['dp'=8,'mp'=4] {'dp'}, use_global_device_ids=true, to_apply=%add.1 | all-reduce | flops 384 | bytes 1536
  309.9 31.6 %all_gather.17 = bf16[2,384,384]{1,2,0:T(8,128)(2,1)S(1)} all-gather(bf16[2,384,48]{1,2,0:T(8,128)(2,1)S(1)} %convert_element_type.103), channel_id=1, replica_groups=mesh['dp'=8,'mp'=4] {'dp'}, dimensions={2}, use_global_device_ids=true | all-gather | bytes 663552 | tf_op jit(solution)/shard_map/all_gather | solution.py:101
  341.5 34.2 %multiply_convert_fusion = (bf16[8192,384]{1,0:T(8,128)(2,1)}, f32[8192,384]{1,0:T(8,128)}, f32[8192,384]{1,0:T(8,128)}) fusion(f32[384]{0:T(512)S(1)} %convert_element_type.105, bf16[8192,384]{0,1:T(8,128)(2,1)} %all-gather.6.cloned.1.call-done, bf16[2,384,384]{1,2,0:T(8,128)(2,1)S(1)} %all_gather.17), kind=kOutput, calls=%fused_computation.55 | convolution fusion | flops 2623537152 | bytes 38045696 | tf_op jit(solution)/shard_map/dot_general | solution.py:150
  389.6 16.3 %fusion.218 = (f32[384]{0:T(512)}, bf16[8192,384]{1,0:T(8,128)(2,1)S(1)}) fusion(f32[8192,384]{1,0:T(8,128)} %get-tuple-element.147, bf16[8192,384]{0,1:T(8,128)(2,1)} %all-gather.8.cloned.1.call-done, bf16[2,384,384]{1,2,0:T(8,128)(2,1)S(1)} %all_gather.17, f32[8192,384]{1,0:T(8,128)} %get-tuple-element.234, f32[384]{0:T(512)S(1)} %convert_element_type.105), kind=kOutput, calls=%fused_computation.302 | convolution fusion | flops 2466250240 | bytes 38047232 | tf_op jit(solution)/shard_map/dot_general | solution.py:158
  444.5 21.7 %all-reduce.3 = f32[384]{0:T(512)S(1)} all-reduce(f32[384]{0:T(512)} %get-tuple-element.235), channel_id=6, replica_groups=mesh['dp'=8,'mp'=4] {'dp'}, use_global_device_ids=true, to_apply=%region_29.30.clone | all-reduce | flops 384 | bytes 3072
  467.5 28.7 %all-reduce.6.cloned.1.call-done = f32[2,384,384]{1,0,2:T(2,128)} async-done(((f32[2,384,384]{1,0,2:T(2,128)}), f32[2,384,384]{1,0,2:T(2,128)}) %all-reduce.6.cloned.1.call-update) | async-done | bytes 1179664
  499.1 98.2 %reduce-scatter.8.cloned.1.call-done = f32[2048,384]{0,1:T(8,128)} async-done(((f32[8192,384]{0,1:T(8,128)}), f32[2048,384]{0,1:T(8,128)}) %reduce-scatter.8.cloned.1.call-update) | async-done | bytes 3145744 | tf_op jit(solution)/shard_map/reduce_scatter | solution.py:163
  604.3 94.7 %reduce-scatter.6.cloned.1.call-done = f32[2048,384]{0,1:T(8,128)} async-done(((f32[8192,384]{0,1:T(8,128)}), f32[2048,384]{0,1:T(8,128)}) %reduce-scatter.6.cloned.1.call-update) | async-done | bytes 3145744 | tf_op jit(solution)/shard_map/reduce_scatter | solution.py:152
  721.9 39.2 %fusion.105 = bf16[512,6,64]{0,2,1:T(8,128)(2,1)} fusion(bf16[2048,6,64]{0,2,1:T(8,128)(2,1)S(1)} %bitcast.165, f32[6,512,2048]{2,1,0:T(8,128)} %fusion.220, pred[512,2048]{1,0:T(8,128)(4,1)} %copy-done.11, f32[6,512]{1,0:T(8,128)S(1)} %log_add_fusion.3, f32[6,512,2048]{2,1,0:T(8,128)} %get-tuple-element.231), kind=kOutput, calls=%fused_computation.136 | convolution fusion | flops 881005568 | bytes 53358592 | tf_op jit(solution)/shard_map/hqk,khd->qhd/dot_general | solution.py:186
  761.1 43.2 %fusion.37 = f32[6,64,2048]{2,1,0:T(8,128)} fusion(bf16[512,6,64]{0,2,1:T(8,128)(2,1)S(1)} %bitcast.195, f32[6,512,2048]{2,1,0:T(8,128)} %fusion.220, pred[512,2048]{1,0:T(8,128)(4,1)} %copy-done.11, f32[6,512,2048]{2,1,0:T(8,128)} %get-tuple-element.231, f32[6,512]{1,0:T(8,128)S(1)} %log_add_fusion.3), kind=kOutput, calls=%fused_computation.73 | convolution fusion | flops 880808960 | bytes 54931456 | tf_op jit(solution)/shard_map/hqk,qhd->khd/dot_general | solution.py:188
  828.7 39.0 %fusion.108 = bf16[512,6,64]{0,2,1:T(8,128)(2,1)} fusion(bf16[2048,6,64]{0,2,1:T(8,128)(2,1)S(1)} %bitcast.166, f32[6,512,2048]{2,1,0:T(8,128)} %fusion.221, pred[512,2048]{1,0:T(8,128)(4,1)} %get-tuple-element.165, f32[6,512]{1,0:T(8,128)S(1)} %copy-done.84, f32[6,512,2048]{2,1,0:T(8,128)} %get-tuple-element.229), kind=kOutput, calls=%fused_computation.137 | convolution fusion | flops 881005568 | bytes 53358592 | tf_op jit(solution)/shard_map/hqk,khd->qhd/dot_general | solution.py:186
  867.7 42.9 %fusion.45 = f32[6,64,2048]{2,1,0:T(8,128)} fusion(bf16[512,6,64]{0,2,1:T(8,128)(2,1)S(1)} %bitcast.193, f32[6,512,2048]{2,1,0:T(8,128)} %fusion.221, pred[512,2048]{1,0:T(8,128)(4,1)} %get-tuple-element.165, f32[6,512,2048]{2,1,0:T(8,128)} %get-tuple-element.229, f32[6,512]{1,0:T(8,128)S(1)} %copy-done.84), kind=kOutput, calls=%fused_computation.75 | convolution fusion | flops 880808960 | bytes 54931456 | tf_op jit(solution)/shard_map/hqk,qhd->khd/dot_general | solution.py:188
  935.2 38.7 %fusion.111 = bf16[512,6,64]{0,2,1:T(8,128)(2,1)} fusion(bf16[2048,6,64]{0,2,1:T(8,128)(2,1)S(1)} %bitcast.167, f32[6,512,2048]{2,1,0:T(8,128)} %fusion.222, pred[512,2048]{1,0:T(8,128)(4,1)} %get-tuple-element.166, f32[6,512]{1,0:T(8,128)S(1)} %copy-done.83, f32[6,512,2048]{2,1,0:T(8,128)} %get-tuple-element.227), kind=kOutput, calls=%fused_computation.138 | convolution fusion | flops 881005568 | bytes 53358592 | tf_op jit(solution)/shard_map/hqk,khd->qhd/dot_general | solution.py:186
  973.9 42.3 %fusion.53 = f32[6,64,2048]{2,1,0:T(8,128)} fusion(bf16[512,6,64]{0,2,1:T(8,128)(2,1)S(1)} %bitcast.191, f32[6,512,2048]{2,1,0:T(8,128)} %fusion.222, pred[512,2048]{1,0:T(8,128)(4,1)} %get-tuple-element.166, f32[6,512,2048]{2,1,0:T(8,128)} %get-tuple-element.227, f32[6,512]{1,0:T(8,128)S(1)} %copy-done.83), kind=kOutput, calls=%fused_computation.77 | convolution fusion | flops 880808960 | bytes 54931456 | tf_op jit(solution)/shard_map/hqk,qhd->khd/dot_general | solution.py:188
  1040.6 39.3 %fusion.114 = bf16[512,6,64]{0,2,1:T(8,128)(2,1)} fusion(bf16[2048,6,64]{0,2,1:T(8,128)(2,1)S(1)} %bitcast.168, f32[6,512,2048]{2,1,0:T(8,128)} %fusion.223, pred[512,2048]{1,0:T(8,128)(4,1)} %get-tuple-element.167, f32[6,512]{1,0:T(8,128)S(1)} %copy-done.82, f32[6,512,2048]{2,1,0:T(8,128)} %get-tuple-element.225), kind=kOutput, calls=%fused_computation.139 | convolution fusion | flops 881005568 | bytes 53358592 | tf_op jit(solution)/shard_map/hqk,khd->qhd/dot_general | solution.py:186
  1096.0 43.3 %add_convert_fusion.1 = bf16[6,64,2048]{2,1,0:T(8,128)(2,1)} fusion(f32[6,64,2048]{2,1,0:T(8,128)} %fusion.53, f32[6,64,2048]{2,1,0:T(8,128)} %fusion.37, f32[6,64,2048]{2,1,0:T(8,128)} %fusion.45, bf16[512,6,64]{0,2,1:T(8,128)(2,1)S(1)} %bitcast.189, f32[6,512,2048]{2,1,0:T(8,128)} %fusion.223, pred[512,2048]{1,0:T(8,128)(4,1)} %get-tuple-element.167, ...), kind=kOutput, calls=%fused_computation.94 | convolution fusion | flops 883954688 | bytes 62795776 | tf_op jit(solution)/shard_map/hqk,qhd->khd/dot_general | solution.py:188
  1182.5 16.5 %scatter_custom_fusion = f32[4950,384]{1,0:T(8,128)} fusion(s32[2048]{0:T(1024)} %get-tuple-element.149, f32[2048,384]{1,0:T(8,128)S(1)} %copy.144, f32[]{:T(128)} %constant.64.clone.1), kind=kCustom, calls=%fused_computation.87 | custom fusion | flops 786432 | bytes 7603712 | tf_op jit(solution)/shard_map/scatter-add | solution.py:216
  1207.2 39.7 %psum.7 = f32[8,384]{1,0:T(8,128)S(1)} all-reduce(f32[8,384]{1,0:T(8,128)S(1)} %stack.35), channel_id=1, replica_groups=mesh['dp'=8,'mp'=4] {'dp','mp'}, use_global_device_ids=true, to_apply=%region_37.38 | all-reduce | flops 3072 | bytes 24576 | tf_op jit(solution)/shard_map/psum | solution.py:238
  (334 shorter events, 384.8 us)
Async XLA Ops:
  7.2 134.5 %all-gather.4.cloned.1.call-start = ((), (), s32[]{:S(2)}) async-start(), calls=%async_computation.3 | async-start | bytes 1216512 | tf_op jit(solution)/shard_map/all_gather | solution.py:99
  8.8 332.7 %all-gather.6.cloned.1.call-start = ((), (), s32[]{:S(2)}) async-start(), calls=%async_computation.4 | async-start | bytes 7864320 | tf_op jit(solution)/shard_map/all_gather | solution.py:149
  18.3 123.4 %copy-start.80 = (f32[384]{0:T(512)}, f32[384]{0:T(512)S(1)}, u32[]{:S(2)}) copy-start(f32[384]{0:T(512)S(1)} %get-tuple-element.123) | copy-start | bytes 4612
  18.3 123.4 %copy-start.94 = (f32[384]{0:T(512)}, f32[384]{0:T(512)S(1)}, u32[]{:S(2)}) copy-start(f32[384]{0:T(512)S(1)} %get-tuple-element.122) | copy-start | bytes 4612
  141.7 124.8 %copy-start.11 = (pred[512,2048]{1,0:T(8,128)(4,1)}, pred[512,2048]{1,0:T(8,128)(4,1)S(1)}, u32[]{:S(2)}) copy-start(pred[512,2048]{1,0:T(8,128)(4,1)S(1)} %get-tuple-element.164) | copy-start | bytes 3145732
  146.2 66.3 %copy-start.33 = (bf16[512,384]{0,1:T(8,128)(2,1)}, bf16[512,384]{0,1:T(8,128)(2,1)S(1)}, u32[]{:S(2)}) copy-start(bf16[512,384]{0,1:T(8,128)(2,1)S(1)} %get-tuple-element.150) | copy-start | bytes 1179652
  146.2 77.3 %copy-start.31 = (bf16[512,384]{0,1:T(8,128)(2,1)}, bf16[512,384]{0,1:T(8,128)(2,1)S(1)}, u32[]{:S(2)}) copy-start(bf16[512,384]{0,1:T(8,128)(2,1)S(1)} %get-tuple-element.153) | copy-start | bytes 1179652
  146.4 77.0 %copy-start = (bf16[2048,384]{0,1:T(8,128)(2,1)}, bf16[2048,384]{0,1:T(8,128)(2,1)S(1)}, u32[]{:S(2)}) copy-start(bf16[2048,384]{0,1:T(8,128)(2,1)S(1)} %get-tuple-element.154) | copy-start | bytes 4718596
  146.4 120.1 %copy-start.4 = (bf16[2048,384]{0,1:T(8,128)(2,1)}, bf16[2048,384]{0,1:T(8,128)(2,1)S(1)}, u32[]{:S(2)}) copy-start(bf16[2048,384]{0,1:T(8,128)(2,1)S(1)} %get-tuple-element.155) | copy-start | bytes 4718596
  284.4 97.8 %all-gather.8.cloned.1.call-start = ((), (), s32[]{:S(2)}) async-start(), calls=%async_computation.6 | async-start | bytes 7864320 | tf_op jit(solution)/shard_map/all_gather | solution.py:157
  285.2 211.0 %all-reduce.6.cloned.1.call-start = ((), (), s32[]{:S(2)}) async-start(), calls=%async_computation.9 | async-start | bytes 2359296
  416.0 181.3 %reduce-scatter.8.cloned.1.call-start = ((), (), s32[]{:S(2)}) async-start(), calls=%async_computation.7 | async-start | bytes 15728640 | tf_op jit(solution)/shard_map/reduce_scatter | solution.py:163
  427.3 271.7 %reduce-scatter.6.cloned.1.call-start = ((), (), s32[]{:S(2)}) async-start(), calls=%async_computation.5 | async-start | bytes 15728640 | tf_op jit(solution)/shard_map/reduce_scatter | solution.py:152
  438.2 159.1 %copy-start.3 = (f32[2048,384]{0,1:T(8,128)S(1)}, f32[2048,384]{0,1:T(8,128)}, u32[]{:S(2)}) copy-start(f32[2048,384]{0,1:T(8,128)} %copy-done.2) | copy-start | bytes 9437188
  438.2 159.1 %copy-start.41 = (f32[2048]{0:T(1024)S(1)}, f32[2048]{0:T(1024)}, u32[]{:S(2)}) copy-start(f32[2048]{0:T(1024)} %copy-done.40) | copy-start | bytes 24580
  438.2 162.3 %copy-start.66 = (f32[2048]{0:T(1024)S(1)}, f32[2048]{0:T(1024)}, u32[]{:S(2)}) copy-start(f32[2048]{0:T(1024)} %copy-done.65) | copy-start | bytes 24580
  438.3 162.3 %copy-start.56 = (f32[2048]{0:T(1024)S(1)}, f32[2048]{0:T(1024)}, u32[]{:S(2)}) copy-start(f32[2048]{0:T(1024)} %copy-done.55) | copy-start | bytes 24580
  438.3 260.7 %copy-start.59 = (pred[2048]{0:T(1024)(128)(4,1)S(1)}, pred[2048]{0:T(1024)(128)(4,1)}, u32[]{:S(2)}) copy-start(pred[2048]{0:T(1024)(128)(4,1)} %copy-done.57) | copy-start | bytes 6148
  438.3 818.6 %reduce-scatter.10.cloned.1.call-start = ((), (), s32[]{:S(2)}) async-start(), calls=%async_computation.8 | async-start | bytes 2433024
  443.1 317.9 %copy-start.75 = (f32[6,512]{1,0:T(8,128)}, f32[6,512]{1,0:T(8,128)S(1)}, u32[]{:S(2)}) copy-start(f32[6,512]{1,0:T(8,128)S(1)} %log_add_fusion.3) | copy-start | bytes 36868
  1182.4 74.5 %copy-start.43 = (f32[384,48]{0,1:T(8,128)S(1)}, f32[384,48]{0,1:T(8,128)}, u32[]{:S(2)}) copy-start(f32[384,48]{0,1:T(8,128)} %param.29) | copy-start | bytes 221188
  1182.4 74.5 %copy-start.67 = (f32[384,48]{0,1:T(8,128)S(1)}, f32[384,48]{0,1:T(8,128)}, u32[]{:S(2)}) copy-start(f32[384,48]{0,1:T(8,128)} %param.41) | copy-start | bytes 221188
  1182.5 74.5 %copy-start.68 = (f32[384,48]{0,1:T(8,128)S(1)}, f32[384,48]{0,1:T(8,128)}, u32[]{:S(2)}) copy-start(f32[384,48]{0,1:T(8,128)} %param.37) | copy-start | bytes 221188
  1182.5 74.4 %copy-start.69 = (f32[384,48]{0,1:T(8,128)S(1)}, f32[384,48]{0,1:T(8,128)}, u32[]{:S(2)}) copy-start(f32[384,48]{0,1:T(8,128)} %param.33) | copy-start | bytes 221188
  (81 other events, 1672.4 us)
Sparse Core Ops, SparseCore 0:
  11.5 56.7 all-gather.3
  284.6 49.0 all-gather.5
  335.8 46.3 all-gather.7
  416.1 80.0 all-reduce.5
  498.8 98.4 reduce-scatter.7
  599.9 99.0 reduce-scatter.5
  1157.8 99.0 reduce-scatter.9
where the time goes:
time: 1270 us
  matrix products  627 us (49%)
  waiting for transfers between devices  238 us (19%)
  other arithmetic  164 us (13%)
  blocking collectives  116 us (9%)
  local copies, waits for them, and re-layouts  102 us (8%)
  between operations  18 us (1%)
    dot_general x4, matrix products, body(): jnp.einsum('hqk,qhd->khd', score_grad, query[lower:lower + block], prefer...  172 us
    dot_general x4, matrix products, body(): jnp.einsum('hqk,khd->qhd', score_grad, key_rows, preferred_element_type=j...  156 us
    reduce_scatter x1, waiting for transfers between devices, body(): lax.psum_scatter(contract_cols(grads_in, w_up), 'mp', scatter_dimension=0...  98.2 us
    reduce_scatter x1, waiting for transfers between devices, body(): lax.psum_scatter(contract_cols(hidden, w_down), 'mp', scatter_dimension=0...  94.7 us
    dot_general x4, matrix products, body(): jnp.einsum('hqk,qhd->khd', probs.astype(jnp.bfloat16), part_grad, preferr...  55.7 us
    dot_general x4, matrix products, body(): jnp.einsum('hqk,khd->qhd', probs_low, value, preferred_element_type=jnp.f...  46.5 us
    unnamed x2, blocking collectives  44.8 us
    dot_general x4, matrix products, block_scores(): jnp.einsum('qhd,khd->hqk', query[lower:lower + block], key_rows, preferre...  43.7 us
  transfers between devices with their start and end apart: 7, of which 5 were waited for; matrix products, arithmetic and copies ran while one was open for 20% of the time, Pallas kernels for 0%

commit v1 on v0

v1 whole, which is shorter than its diff:
```python
import functools
import math

import jax
import jax.numpy as jnp
from jax import lax
from jax.experimental import pallas as pl
from jax.experimental.pallas import tpu as pltpu
from jax.sharding import PartitionSpec as P

HEADS = 6
HEAD = 64
PAIR = 2 * HEAD
PAIRS = HEADS // 2
BLK = 128
REACH = 5
EXCLUDED = -8.0e9
INCLUDED = 3.0e38

NORM_EPS = 1e-06
BETA_ONE = 0.9
BETA_TWO = 0.999
ADAM_EPS = 1e-08
MATRIX_RATE = 0.05
VECTOR_RATE = 0.2
WEIGHT_DECAY = 0.05
AVERAGE_DECAY = 0.8

LOG2E = 1.4426950408889634
SCORE_LOG2 = LOG2E / math.sqrt(HEAD)
SCALE = 1.0 / math.sqrt(HEAD)

f32 = jnp.float32
bf16 = jnp.bfloat16
NN = (((1,), (0,)), ((), ()))
NT = (((1,), (1,)), ((), ()))
TN = (((0,), (0,)), ((), ()))
VM = pl.BlockSpec(memory_space=pltpu.VMEM)
SM = pl.BlockSpec(memory_space=pltpu.SMEM)
S = jax.ShapeDtypeStruct


def dot(left, right, dims=NN):
    return lax.dot_general(left, right, dims, preferred_element_type=f32)


def kernel_call(body, ins, outs, scratch=(), flops=0, moved=0, name=None):
    return pl.pallas_call(
        body,
        out_shape=outs,
        in_specs=ins,
        out_specs=tuple(VM for _ in outs),
        scratch_shapes=list(scratch),
        compiler_params=pltpu.CompilerParams(vmem_limit_bytes=58 * 2**20),
        cost_estimate=pl.CostEstimate(flops=flops, bytes_accessed=moved, transcendentals=0),
        name=name,
    )


def row_sums(values):
    rows, width = values.shape
    return jnp.sum(values.reshape(rows // 8, 8, width), axis=0)


def norm_parts(values):
    scale = 1.0 / values.shape[-1]
    centre = jnp.sum(values, axis=-1, keepdims=True) * scale
    centred = values - centre
    spread = jnp.sum(centred * centred, axis=-1, keepdims=True) * scale
    inverse = lax.rsqrt(spread + NORM_EPS)
    return centred * inverse, inverse


def norm_back(unit, inverse, gain, grad):
    scale = 1.0 / unit.shape[-1]
    scaled = grad * gain
    mean = jnp.sum(scaled, axis=-1, keepdims=True) * scale
    along = jnp.sum(scaled * unit, axis=-1, keepdims=True) * scale
    return inverse * (scaled - mean - unit * along)


def tile_rows(count, size):
    return pl.ds(pl.multiple_of(count * size, size), size)


def pack_body(win, offs, images, keep, seg_rows, vec, packed, normed, normed_t, seg_cols, acc, slots):
    images_here, length = keep.shape
    rows, width = packed.shape
    before = lax.broadcasted_iota(jnp.int32, (length, length), 0)
    after = lax.broadcasted_iota(jnp.int32, (length, length), 1)
    tri = jnp.where(before <= after, 1.0, 0.0).astype(bf16)
    kept = keep[...]
    ranks = dot(kept.astype(f32).astype(bf16), tri).astype(jnp.int32) - 1
    slots[...] = jnp.where(kept > 0, ranks, -4 * win)
    acc[0:8, :] = jnp.zeros((8, width), f32)
    place = lax.broadcasted_iota(jnp.int32, (win, length), 0)

    def one_image(i, carry):
        base = pl.multiple_of((offs[i] // 8) * 8, 8)
        shift = offs[i] - base
        chosen = jnp.where(place == slots[pl.ds(i, 1), :] + shift, 1.0, 0.0).astype(bf16)
        moved = dot(chosen, images[i])
        acc[pl.ds(base, 8), :] += moved[0:8]
        acc[pl.ds(base + 8, win - 8), :] = moved[8:]
        return carry

    lax.fori_loop(0, images_here, one_image, 0)

    def one_tile(i, carry):
        sl = tile_rows(i, 256)
        values = acc[sl, :]
        packed[sl, :] = values.astype(bf16)
        unit, _ = norm_parts(values)
        low = (unit * vec[0:1, :] + vec[1:2, :]).astype(bf16)
        normed[sl, :] = low
        normed_t[:, sl] = low.T
        return carry

    lax.fori_loop(0, rows // 256, one_tile, 0)

    def one_block(j, carry):
        line = seg_rows[pl.ds(j, 1), :]
        seg_cols[tile_rows(j, BLK), :] = jnp.broadcast_to(line, (BLK, BLK)).T
        return carry

    lax.fori_loop(0, rows // BLK, one_block, 0)


def pack_call(images, keep, offs, seg_rows, vec, rows):
    images_here, length, width = images.shape
    win = (length + 7 + 7) // 8 * 8
    return kernel_call(
        functools.partial(pack_body, win),
        [SM, VM, VM, VM, VM],
        (S((rows, width), bf16), S((rows, width), bf16), S((width, rows), bf16), S((rows, BLK), jnp.int32)),
        [pltpu.VMEM((rows + win, width), f32), pltpu.VMEM((images_here, length), jnp.int32)],
        flops=2 * images_here * win * length * width,
        moved=images.size * 2 + rows * width * 6,
        name="pack",
    )(offs, images, keep, seg_rows, vec)


def window(seg, offs, counts, j, images_here, rows):
    first = seg[j * BLK]
    last = seg[j * BLK + BLK - 1]
    used = last < images_here
    last_here = jnp.where(used, last, 0)
    low = offs[first] // BLK
    end = jnp.where(used, offs[last_here] + counts[last_here], rows)
    return low, (end + BLK - 1) // BLK - low


def masked_pair(pair):
    lane = lax.broadcasted_iota(jnp.int32, pair.shape, 1)
    none = jnp.zeros_like(pair)
    return jnp.concatenate([jnp.where(lane < HEAD, pair, none), jnp.where(lane >= HEAD, pair, none)], axis=0)


def limits(seg_rows, seg_cols, j, keys):
    same = seg_cols[keys, :] == seg_rows[pl.ds(j, 1), :]
    lim = jnp.where(same, INCLUDED, EXCLUDED)
    return jnp.concatenate([lim, lim], axis=1)


def over_windows(seg, offs, counts, images_here, rows, block):
    def one(j, carry):
        low, size = window(seg, offs, counts, j, images_here, rows)
        for n in range(1, REACH + 1):

            @pl.when(size == n)
            def _():
                block(j, pl.ds(pl.multiple_of(low * BLK, BLK), n * BLK))

        return carry

    lax.fori_loop(0, rows // BLK, one, 0)


def attend_body(seg, offs, counts, normed, w_t, bias, seg_rows, seg_cols, qkv, mixed_t, stats, value_t):
    rows, width = normed.shape
    images_here = offs.shape[0]

    def project(i, carry):
        sl = tile_rows(i, 512)
        low = (dot(normed[sl, :], w_t[...], NT) + bias[...]).astype(bf16)
        qkv[sl, :] = low
        value_t[:, sl] = low[:, 2 * width :].T
        return carry

    lax.fori_loop(0, rows // 512, project, 0)

    def block(j, keys):
        here = tile_rows(j, BLK)
        lim = limits(seg_rows, seg_cols, j, keys)
        for p in range(PAIRS):
            at = slice(p * PAIR, (p + 1) * PAIR)
            queries = masked_pair(qkv[here, at])
            scores = dot(qkv[keys, width + p * PAIR : width + (p + 1) * PAIR], queries, NT)
            scores = jnp.minimum(scores, lim)
            top = jnp.max(scores, axis=0, keepdims=True)
            expo = jnp.exp2((scores - top) * SCORE_LOG2)
            total = jnp.sum(expo, axis=0, keepdims=True)
            probs_low = (expo * (1.0 / total)).astype(bf16)
            out = dot(value_t[at, keys], probs_low)
            mixed_t[p * PAIR : p * PAIR + HEAD, here] = out[:HEAD, :BLK].astype(bf16)
            mixed_t[p * PAIR + HEAD : (p + 1) * PAIR, here] = out[HEAD:, BLK:].astype(bf16)
            level = top * SCORE_LOG2 + jnp.log2(total)
            stats[pl.ds(j, 1), p * 2 * BLK : (p + 1) * 2 * BLK] = level

    over_windows(seg, offs, counts, images_here, rows, block)


def attend_call(seg, offs, counts, normed, w_t, bias, seg_rows, seg_cols):
    rows, width = normed.shape
    return kernel_call(
        attend_body,
        [SM, SM, SM, VM, VM, VM, VM, VM],
        (S((rows, 3 * width), bf16), S((width, rows), bf16), S((rows // BLK, HEADS * BLK), f32)),
        [pltpu.VMEM((width, rows), bf16)],
        flops=2 * rows * width * 3 * width + 4 * rows * 384 * width,
        moved=rows * width * 12,
        name="attend",
    )(seg, offs, counts, normed, w_t, bias, seg_rows, seg_cols)


def attend_back_body(seg, offs, counts, qkv, mixed_grad, stats, seg_rows, seg_cols, qkv_grad, key_t, key_grad, value_grad):
    rows, width = mixed_grad.shape
    images_here = offs.shape[0]

    def prepare(i, carry):
        sl = tile_rows(i, 512)
        key_t[:, sl] = qkv[sl, width : 2 * width].T
        key_grad[sl, :] = jnp.zeros((512, width), f32)
        value_grad[sl, :] = jnp.zeros((512, width), f32)
        return carry

    lax.fori_loop(0, rows // 512, prepare, 0)

    def block(j, keys):
        here = tile_rows(j, BLK)
        lim = limits(seg_rows, seg_cols, j, keys)
        for p in range(PAIRS):
            at = slice(p * PAIR, (p + 1) * PAIR)
            queries = masked_pair(qkv[here, at])
            outs = masked_pair(mixed_grad[here, at])
            level = stats[pl.ds(j, 1), p * 2 * BLK : (p + 1) * 2 * BLK]
            scores = dot(qkv[keys, width + p * PAIR : width + (p + 1) * PAIR], queries, NT)
            probs = jnp.exp2(jnp.minimum(scores, lim) * SCORE_LOG2 - level)
            prob_grad = dot(qkv[keys, 2 * width + p * PAIR : 2 * width + (p + 1) * PAIR], outs, NT)
            inner = jnp.sum(probs * prob_grad, axis=0, keepdims=True)
            score_grad = (probs * (prob_grad - inner)).astype(bf16)
            key_grad[keys, at] += dot(score_grad, queries)
            value_grad[keys, at] += dot(probs.astype(bf16), outs)
            query_t = dot(key_t[at, keys], score_grad) * SCALE
            joined = jnp.concatenate([query_t[:HEAD, :BLK], query_t[HEAD:, BLK:]], axis=0)
            qkv_grad[here, at] = joined.T.astype(bf16)

    over_windows(seg, offs, counts, images_here, rows, block)

    def finish(i, carry):
        sl = tile_rows(i, 256)
        qkv_grad[sl, width : 2 * width] = (key_grad[sl, :] * SCALE).astype(bf16)
        qkv_grad[sl, 2 * width :] = value_grad[sl, :].astype(bf16)
        return carry

    lax.fori_loop(0, rows // 256, finish, 0)


def attend_back_call(seg, offs, counts, qkv, mixed_grad, stats, seg_rows, seg_cols):
    rows, width = mixed_grad.shape
    return kernel_call(
        attend_back_body,
        [SM, SM, SM, VM, VM, VM, VM, VM],
        (S((rows, 3 * width), bf16),),
        [pltpu.VMEM((width, rows), bf16), pltpu.VMEM((rows, width), f32), pltpu.VMEM((rows, width), f32)],
        flops=10 * rows * 384 * width,
        moved=rows * width * 16,
        name="attend_back",
    )(seg, offs, counts, qkv, mixed_grad, stats, seg_rows, seg_cols)[0]


def feed_body(
    packed, mixed_t, cot, vec, up_bias, w_out_t, w_up_t, w_down,
    layer_out, middle_grad, mixed_grad, out_grad, ffn_grad, bias_grad, sums,
    hid_s, gi_s, n2t_s, glt_s, mlow_s,
):
    rows, width = packed.shape
    size = 512
    bias_grad[...] = jnp.zeros_like(bias_grad)
    sums[...] = jnp.zeros_like(sums)

    def one(i, carry):
        sl = tile_rows(i, size)
        middle = packed[sl, :].astype(f32) + dot(mixed_t[:, sl].T, w_out_t[...], NT) + vec[4:5, :]
        unit, inverse = norm_parts(middle)
        low = (unit * vec[5:6, :] + vec[6:7, :]).astype(bf16)
        n2t_s[:, sl] = low.T
        valid = lax.broadcasted_iota(jnp.int32, (size, 1), 0) + i * size < rows - 1
        grad_out = jnp.where(valid, cot[sl, :].astype(f32), 0.0)
        grad_low = grad_out.astype(bf16)
        glt_s[:, sl] = grad_low.T
        sums[24:32, :] += row_sums(grad_out)
        u = dot(low, w_up_t[...], NT) + up_bias[...]
        phi = 0.5 + 0.5 * lax.erf(u * (1.0 / math.sqrt(2.0)))
        hidden = (u * phi).astype(bf16)
        hid_s[sl, :] = hidden
        slope = phi + u * jnp.exp2(u * u * (-0.5 * LOG2E)) * (1.0 / math.sqrt(2.0 * math.pi))
        grad_in = dot(grad_low, w_down[...], NT) * slope
        bias_grad[...] += row_sums(grad_in)
        grad_in_low = grad_in.astype(bf16)
        gi_s[sl, :] = grad_in_low
        down = dot(hidden, w_down[...])
        layer_out[sl, :] = jnp.where(valid, middle + down + vec[7:8, :], 0.0).astype(bf16)
        n2_grad = dot(grad_in_low, w_up_t[...])
        sums[8:16, :] += row_sums(n2_grad * unit)
        sums[16:24, :] += row_sums(n2_grad)
        total = grad_out + norm_back(unit, inverse, vec[5:6, :], n2_grad)
        middle_grad[sl, :] = total
        sums[0:8, :] += row_sums(total)
        total_low = total.astype(bf16)
        mlow_s[sl, :] = total_low
        mixed_grad[sl, :] = dot(total_low, w_out_t[...]).astype(bf16)
        return carry

    lax.fori_loop(0, rows // size, one, 0)
    units = w_up_t.shape[0]
    for lower in range(0, units, 256):
        hs = slice(lower, lower + 256)
        ffn_grad[0, hs, :] = dot(n2t_s[...], gi_s[:, hs]).T
        ffn_grad[1, hs, :] = dot(glt_s[...], hid_s[:, hs]).T
    out_grad[...] = dot(mixed_t[...], mlow_s[...]).T


def feed_call(packed, mixed_t, cot, vec, up_bias, w_out_t, w_up_t, w_down):
    rows, width = packed.shape
    units = w_up_t.shape[0]
    return kernel_call(
        feed_body,
        [VM] * 8,
        (
            S((rows, width), bf16),
            S((rows, width), f32),
            S((rows, width), bf16),
            S((width, width), f32),
            S((2, units, width), f32),
            S((8, units), f32),
            S((32, width), f32),
        ),
        [
            pltpu.VMEM((rows, units), bf16),
            pltpu.VMEM((rows, units), bf16),
            pltpu.VMEM((width, rows), bf16),
            pltpu.VMEM((width, rows), bf16),
            pltpu.VMEM((rows, width), bf16),
        ],
        flops=12 * rows * width * units + 6 * rows * width * width,
        moved=rows * width * 16 + units * width * 12,
        name="feed",
    )(packed, mixed_t, cot, vec, up_bias, w_out_t, w_up_t, w_down)


def input_body(qkv_grad, w_t, packed, normed_t, middle_grad, vec, input_grad, weight_grad, sums):
    rows, width = packed.shape
    size = 512
    sums[...] = jnp.zeros_like(sums)

    def one(i, carry):
        sl = tile_rows(i, size)
        grads = qkv_grad[sl, :]
        normed_grad = dot(grads, w_t[...])
        unit, inverse = norm_parts(packed[sl, :].astype(f32))
        sums[0:8, :] += row_sums(normed_grad * unit)
        sums[8:16, :] += row_sums(normed_grad)
        sums[16:24, :] += row_sums(grads[:, :width].astype(f32))
        sums[24:32, :] += row_sums(grads[:, 2 * width :].astype(f32))
        input_grad[sl, :] = middle_grad[sl, :] + norm_back(unit, inverse, vec[0:1, :], normed_grad)
        return carry

    lax.fori_loop(0, rows // size, one, 0)
    for lower in range(0, 3 * width, 128):
        hs = slice(lower, lower + 128)
        weight_grad[hs, :] = dot(normed_t[...], qkv_grad[:, hs]).T


def input_call(qkv_grad, w_t, packed, normed_t, middle_grad, vec):
    rows, width = packed.shape
    return kernel_call(
        input_body,
        [VM] * 6,
        (S((rows, width), f32), S((3 * width, width), f32), S((32, width), f32)),
        flops=12 * rows * width * width,
        moved=rows * width * 20,
        name="input_back",
    )(qkv_grad, w_t, packed, normed_t, middle_grad, vec)


def unpack_body(win, offs, keep, input_grad, image_grads, slots):
    images_here, length = keep.shape
    rows, width = input_grad.shape
    before = lax.broadcasted_iota(jnp.int32, (length, length), 0)
    after = lax.broadcasted_iota(jnp.int32, (length, length), 1)
    tri = jnp.where(before <= after, 1.0, 0.0).astype(bf16)
    kept = keep[...]
    ranks = dot(kept.astype(f32).astype(bf16), tri).astype(jnp.int32) - 1
    slots[...] = jnp.where(kept > 0, ranks, -4 * win)
    place = lax.broadcasted_iota(jnp.int32, (win, length), 0)

    def one_image(i, carry):
        base = pl.multiple_of(jnp.minimum((offs[i] // 8) * 8, rows - win), 8)
        shift = offs[i] - base
        chosen = jnp.where(place == slots[pl.ds(i, 1), :] + shift, 1.0, 0.0).astype(bf16)
        values = input_grad[pl.ds(base, win), :]
        high = values.astype(bf16)
        rest = (values - high.astype(f32)).astype(bf16)
        image_grads[i] = dot(chosen, high, TN) + dot(chosen, rest, TN)
        return carry

    lax.fori_loop(0, images_here, one_image, 0)


def unpack_call(offs, keep, input_grad):
    images_here, length = keep.shape
    rows, width = input_grad.shape
    win = (length + 7 + 7) // 8 * 8
    return kernel_call(
        functools.partial(unpack_body, win),
        [SM, VM, VM],
        (S((images_here, length, width), f32),),
        [pltpu.VMEM((images_here, length), jnp.int32)],
        flops=4 * images_here * win * length * width,
        moved=images_here * length * width * 4 + rows * width * 4,
        name="unpack",
    )(offs, keep, input_grad)[0]


def adamw(weight, grad, first, second, average, count, rate, decay):
    first_new = BETA_ONE * first + (1.0 - BETA_ONE) * grad
    second_new = BETA_TWO * second + (1.0 - BETA_TWO) * grad * grad
    first_hat = first_new / (1.0 - jnp.power(BETA_ONE, count))
    second_hat = second_new / (1.0 - jnp.power(BETA_TWO, count))
    weight_new = weight - rate * (first_hat / (jnp.sqrt(second_hat) + ADAM_EPS) + decay * weight)
    average_new = AVERAGE_DECAY * average + (1.0 - AVERAGE_DECAY) * weight_new
    return (weight_new, first_new, second_new, average_new)


def body(
    images, keep_mask, kept_counts, pack_offsets, segment_ids, cotangent,
    attn_weight, ffn_weight, up_bias, vectors,
    attn_first, ffn_first, bias_first, vec_first,
    attn_second, ffn_second, bias_second, vec_second,
    attn_average, ffn_average, bias_average, vec_average, step,
):
    width = images.shape[2]
    rows = segment_ids.shape[0]
    both = ("dp", "mp")
    attn_t = lax.all_gather(attn_weight.astype(bf16).T, both, axis=0, tiled=True)
    ffn_t = lax.all_gather(jnp.swapaxes(ffn_weight.astype(bf16), 1, 2), both, axis=1, tiled=True)
    bias_full = lax.all_gather(up_bias.astype(bf16), both, axis=0, tiled=True).astype(f32)[None, :]
    seg_rows = segment_ids.reshape(rows // BLK, BLK)
    packed, normed, normed_t, seg_cols = pack_call(images, keep_mask, pack_offsets, seg_rows, vectors, rows)
    w_qkv_t = attn_t[: 3 * width]
    w_out_t = attn_t[3 * width :]
    qkv_bias = jnp.concatenate([vectors[2], jnp.zeros_like(vectors[2]), vectors[3]])[None, :]
    qkv, mixed_t, stats = attend_call(
        segment_ids, pack_offsets, kept_counts, normed, w_qkv_t, qkv_bias, seg_rows, seg_cols
    )
    layer_out, middle_grad, mixed_grad, out_grad, ffn_part, bias_part, sums_two = feed_call(
        packed, mixed_t, cotangent, vectors, bias_full, w_out_t, ffn_t[0], ffn_t[1]
    )
    qkv_grad = attend_back_call(
        segment_ids, pack_offsets, kept_counts, qkv, mixed_grad, stats, seg_rows, seg_cols
    )
    input_grad, qkv_weight_grad, sums_one = input_call(qkv_grad, w_qkv_t, packed, normed_t, middle_grad, vectors)
    image_grads = unpack_call(pack_offsets, keep_mask, input_grad)
    sums_one = sums_one.reshape(4, 8, width).sum(axis=1)
    sums_two = sums_two.reshape(4, 8, width).sum(axis=1)
    vec_terms = jnp.concatenate([sums_one, sums_two], axis=0)
    attn_terms = jnp.concatenate([qkv_weight_grad, out_grad], axis=0)
    attn_grad = lax.psum_scatter(attn_terms.astype(bf16), both, scatter_dimension=0, tiled=True).astype(f32).T
    ffn_grad = jnp.swapaxes(
        lax.psum_scatter(ffn_part.astype(bf16), both, scatter_dimension=1, tiled=True).astype(f32), 1, 2
    )
    bias_grad = lax.psum_scatter(bias_part.sum(axis=0), both, scatter_dimension=0, tiled=True)
    vec_grad = lax.psum(vec_terms, both)
    count = step[0].astype(f32)
    attn_up = adamw(
        attn_weight, attn_grad, attn_first, attn_second, attn_average, count, MATRIX_RATE, WEIGHT_DECAY
    )
    ffn_up = adamw(ffn_weight, ffn_grad, ffn_first, ffn_second, ffn_average, count, MATRIX_RATE, WEIGHT_DECAY)
    bias_up = adamw(up_bias, bias_grad, bias_first, bias_second, bias_average, count, VECTOR_RATE, 0.0)
    vec_up = adamw(vectors, vec_grad, vec_first, vec_second, vec_average, count, VECTOR_RATE, 0.0)
    news = [part[k] for k in range(4) for part in (attn_up, ffn_up, bias_up, vec_up)]
    return (layer_out, image_grads, attn_grad, ffn_grad, bias_grad, vec_grad, *news)


def solution(mesh):
    both = ("dp", "mp")
    matrix, slab, line = P(None, both), P(None, None, both), P(both)
    states = (matrix, slab, line, P())
    return jax.shard_map(
        body,
        mesh=mesh,
        in_specs=(P(both, None, None), P(both, None), line, line, line, P(both, None), *states * 4, P()),
        out_specs=(P(both, None), P(both, None, None), *states, *states * 4),
        check_vma=False,
    )
```

time: 1270 us -> 422 us (0.33)
  matrix products: 627 us -> 0 us
  other arithmetic: 164 us -> 15.3 us
  Pallas kernels: 0 us -> 139 us
  local copies, waits for them, and re-layouts: 102 us -> 9.5 us
  waiting for transfers between devices: 238 us -> 162 us
  blocking collectives: 116 us -> 80.8 us
    dot_general x36 -> x0, matrix products: 627 us -> none  [the longest x4 172 us: body(): jnp.einsum('hqk,qhd->khd', score_grad, query[lower:lower + block], prefer...]
    pallas_call x0 -> x6, Pallas kernels: none -> 139 us  [the longest x1 33.3 us: attend_back_call(): kernel_call(attend_back_body, [SM, SM, SM, VM, VM, VM, VM, VM], (S((rows,...]
    reduce_sum x11 -> x3, other arithmetic: 67.2 us -> 0.07 us  [the longest x1 0.03 us: body(): sums_one = sums_one.reshape(4, 8, width).sum(axis=1)]
    reduce_scatter x2, waiting for transfers between devices: 193 us -> 139 us  [the longest x1 102 us: body(): lax.psum_scatter(ffn_part.astype(bf16), both, scatter_dimension=1, tiled=...]
    psum x1 -> x0, blocking collectives: 39.7 us -> none  [body(): vec_grad = lax.psum(vec_terms, ('dp', 'mp'))]
    unnamed x9 -> x4, waiting for transfers between devices: 38.8 us -> 0.07 us
    gather x7 -> x0, local copies, waits for them, and re-layouts: 37 us -> none  [the longest x1 16.6 us: pack_rows(): source = owner * length + position[owner, local]]
    unnamed x207 -> x44, local copies, waits for them, and re-layouts: 37 us -> 0.3 us
  transfers between devices with their start and end apart: 7 -> 4, of which waited for: 5 -> 3; matrix products, arithmetic and copies ran while one was open for 20% -> 4% of each run, Pallas kernels for 0% -> 14%
where the time goes in v1:
time: 422 us; the launch traced here: 421 us
  waiting for transfers between devices  162 us (38%)
  Pallas kernels  139 us (33%)
  blocking collectives  80.8 us (19%)
  other arithmetic  15.3 us (4%)
  between operations  14.8 us (4%)
  local copies, waits for them, and re-layouts  9.5 us (2%)
    reduce_scatter x1, waiting for transfers between devices, body(): lax.psum_scatter(ffn_part.astype(bf16), both, scatter_dimension=1, tiled=...  102 us
    unnamed x2, blocking collectives  80.8 us
    reduce_scatter x1, waiting for transfers between devices, body(): lax.psum_scatter(attn_terms.astype(bf16), both, scatter_dimension=0, tile...  37.6 us
    pallas_call x1, Pallas kernels, attend_back_call(): kernel_call(attend_back_body, [SM, SM, SM, VM, VM, VM, VM, VM], (S((rows,...  33.3 us
    pallas_call x1, Pallas kernels, attend_call(): kernel_call(attend_body, [SM, SM, SM, VM, VM, VM, VM, VM], (S((rows, 3 *...  32.4 us
    pallas_call x1, Pallas kernels, feed_call(): kernel_call(feed_body, [VM] * 8, (S((rows, width), bf16), S((rows, width)...  32.3 us
    all_gather x1, waiting for transfers between devices, body(): lax.all_gather(jnp.swapaxes(ffn_weight.astype(bf16), 1, 2), both, axis=1,...  22.4 us
    pallas_call x1, Pallas kernels, pack_call(): kernel_call(functools.partial(pack_body, win), [SM, VM, VM, VM, VM], (S((...  14 us
  transfers between devices with their start and end apart: 4, of which 3 were waited for; matrix products, arithmetic and copies ran while one was open for 4% of the time, Pallas kernels for 14%

profile of v1, /device:TPU:0, one launch (start us, length us, event | category | flops | bytes accessed | tf_op | source)
XLA Modules:
  0.0 421.3 jit_solution(14755113375461291359)
XLA Ops:
  7.2 1.5 convert_bitcast_fusion.3
  8.8 1.6 convert_bitcast_fusion.2
  10.5 0.8 slice_reduce_fusion.1
  11.9 0.7 convert_element_type.21
  12.7 42.1 %all-reduce = bf16[1536]{0:T(1024)(128)(2,1)S(1)} all-reduce(bf16[1536]{0:T(1024)(128)(2,1)S(1)} %dynamic-update-slice), channel_id=1, replica_groups=mesh['dp'=8,'mp'=4] {'dp','mp'}, use_global_device_ids=true, to_apply=%add | all-reduce | flops 1536 | bytes 6144
  55.4 14.0 %pack.1 = (bf16[2048,384]{1,0:T(8,128)(2,1)}, bf16[2048,384]{1,0:T(8,128)(2,1)}, bf16[384,2048]{1,0:T(8,128)(2,1)}, s32[2048,128]{1,0:T(8,128)}) custom-call(s32[25]{0:T(128)} %offs.7, bf16[25,198,384]{2,1,0:T(8,128)(2,1)} %images.1, s32[25,198]{1,0:T(8,128)} %keep.3, s32[16,128]{1,0:T(8,128)} %bitcast.21, f32[8,384]{1,0:T(8,128)} %vec.5), custom_call_target="tpu_custom_call" | custom-call | flops 790732800 | bytes 8520192 | tf_op jit(solution)/shard_map/pack/pallas_call | solution.py:132
  69.5 2.2 slice.24.w_t
  71.7 1.7 slice.25.w_out_t
  73.4 32.4 %attend.1 = (bf16[2048,1152]{1,0:T(8,128)(2,1)}, bf16[384,2048]{1,0:T(8,128)(2,1)}, f32[16,768]{1,0:T(8,128)}) custom-call(s32[2048]{0:T(1024)} %seg.3, s32[25]{0:T(128)} %offs.7, s32[25]{0:T(128)} %counts.3, bf16[2048,384]{1,0:T(8,128)(2,1)} %get-tuple-element.40.normed, bf16[1152,384]{1,0:T(8,128)(2,1)} %slice.24.w_t, f32[1,1152]{1,0:T(1,128)} %broadcast_in_dim.12.bias, ...), custom_call_target="tpu_custom_call" | custom-call | flops 3019898880 | bytes 9437184 | tf_op jit(solution)/shard_map/attend/pallas_call | solution.py:215
  105.7 22.4 %all-gather.5.cloned.1.call-done = bf16[2,1536,384]{2,1,0:T(8,128)(2,1)} async-done(((bf16[2,48,384]{2,1,0:T(8,128)(2,1)}), bf16[2,1536,384]{2,1,0:T(8,128)(2,1)}) %all-gather.5.cloned.1.call-update) | async-done | bytes 2359312 | tf_op jit(solution)/shard_map/all_gather | solution.py:457
  128.2 3.3 slice_bitcast_fusion
  131.5 32.3 %feed.1 = (bf16[2048,384]{1,0:T(8,128)(2,1)}, f32[2048,384]{1,0:T(8,128)}, bf16[2048,384]{1,0:T(8,128)(2,1)}, f32[384,384]{1,0:T(8,128)}, f32[2,1536,384]{2,1,0:...) custom-call(bf16[2048,384]{1,0:T(8,128)(2,1)} %get-tuple-element.39.packed, bf16[384,2048]{1,0:T(8,128)(2,1)} %get-tuple-element.42.mixed_t, ...), custom_call_target="tpu_custom_call" | custom-call | flops 16307453952 | bytes 19660800 | tf_op jit(solution)/shard_map/feed/pallas_call | solution.py:337
  163.8 33.3 %attend_back.1.qkv_grad = bf16[2048,1152]{1,0:T(8,128)(2,1)} custom-call(s32[2048]{0:T(1024)} %seg.3, s32[25]{0:T(128)} %offs.7, s32[25]{0:T(128)} %counts.3, bf16[2048,1152]{1,0:T(8,128)(2,1)} %get-tuple-element.44.qkv, bf16[2048,384]{1,0:T(8,128)(2,1)} %get-tuple-element.45.mixed_grad, f32[16,768]{1,0:T(8,128)} %get-tuple-element.46.stats, ...), custom_call_target="tpu_custom_call" | custom-call | flops 3019898880 | bytes 12582912 | tf_op jit(solution)/shard_map/attend_back/pallas_call | solution.py:271
  197.1 14.0 %input_back.1 = (f32[2048,384]{1,0:T(8,128)}, f32[1152,384]{1,0:T(8,128)}, f32[32,384]{1,0:T(8,128)}) custom-call(bf16[2048,1152]{1,0:T(8,128)(2,1)} %attend_back.1.qkv_grad, bf16[1152,384]{1,0:T(8,128)(2,1)} %slice.24.w_t, bf16[2048,384]{1,0:T(8,128)(2,1)} %get-tuple-element.39.packed, bf16[384,2048]{1,0:T(8,128)(2,1)} %get-tuple-element.47.normed_t, ...), custom_call_target="tpu_custom_call" | custom-call | flops 3623878656 | bytes 15728640 | tf_op jit(solution)/shard_map/input_back/pallas_call | solution.py:387
  211.0 1.6 convert.9
  212.7 1.2 pad_maximum_fusion
  214.0 4.0 convert_element_type.23
  219.0 38.7 %all-reduce.2 = (f32[1536]{0:T(1024)S(1)}, f32[8,384]{1,0:T(8,128)S(1)}) all-reduce(f32[1536]{0:T(1024)S(1)} %reduce_sum.27, f32[8,384]{1,0:T(8,128)S(1)} %pad_maximum_fusion.1), channel_id=4, replica_groups=mesh['dp'=8,'mp'=4] {'dp','mp'}, use_global_device_ids=true, to_apply=%region_3.0.clone | all-reduce | flops 4608 | bytes 36864
  257.8 13.0 %unpack.1 = f32[25,198,384]{2,1,0:T(8,128)} custom-call(s32[25]{0:T(128)} %offs.7, s32[25,198]{1,0:T(8,128)} %keep.3, f32[2048,384]{1,0:T(8,128)} %get-tuple-element.49.input_grad), custom_call_target="tpu_custom_call" | custom-call | flops 1581465600 | bytes 10748928 | tf_op jit(solution)/shard_map/unpack/pallas_call | solution.py:425
  271.5 0.6 multiply_add_fusion.4
  272.1 37.6 %reduce-scatter.3.cloned.1.call-done = bf16[48,384]{1,0:T(8,128)(2,1)} async-done(((bf16[1536,384]{1,0:T(8,128)(2,1)}), bf16[48,384]{1,0:T(8,128)(2,1)}) %reduce-scatter.3.cloned.1.call-update) | async-done | bytes 36880 | tf_op jit(solution)/shard_map/reduce_scatter | solution.py:479
  309.7 1.5 multiply_add_fusion.2
  311.2 101.7 %reduce-scatter.5.cloned.1.call-done = bf16[2,48,384]{2,1,0:T(8,128)(2,1)} async-done(((bf16[2,1536,384]{2,1,0:T(8,128)(2,1)}), bf16[2,48,384]{2,1,0:T(8,128)(2,1)}) %reduce-scatter.5.cloned.1.call-update) | async-done | bytes 73744 | tf_op jit(solution)/shard_map/reduce_scatter | solution.py:481
  413.0 1.8 multiply_add_fusion
  (63 shorter events, 2.5 us)
Async XLA Ops:
  7.2 62.3 %all-gather.3.cloned.1.call-start = ((), (), s32[]{:S(2)}) async-start(), calls=%async_computation.2 | async-start | bytes 1216512 | tf_op jit(solution)/shard_map/all_gather | solution.py:456
  8.8 119.4 %all-gather.5.cloned.1.call-start = ((), (), s32[]{:S(2)}) async-start(), calls=%async_computation.3 | async-start | bytes 2433024 | tf_op jit(solution)/shard_map/all_gather | solution.py:457
  10.4 299.3 %reduce-scatter.3.cloned.1.call-start = ((), (), s32[]{:S(2)}) async-start(), calls=%async_computation.4 | async-start | bytes 1216512 | tf_op jit(solution)/shard_map/reduce_scatter | solution.py:479
  211.0 1.6 copy-start.1
  213.9 199.0 %reduce-scatter.5.cloned.1.call-start = ((), (), s32[]{:S(2)}) async-start(), calls=%async_computation.5 | async-start | bytes 2433024 | tf_op jit(solution)/shard_map/reduce_scatter | solution.py:481
  218.0 0.8 copy-start.12
  218.0 0.9 copy-start.10
  257.6 13.8 %copy-start.16 = (f32[8,384]{1,0:T(8,128)}, f32[8,384]{1,0:T(8,128)S(1)}, u32[]{:S(2)}) copy-start(f32[8,384]{1,0:T(8,128)S(1)} %get-tuple-element.59) | copy-start | bytes 36868
  257.6 13.2 %copy-start.17 = (f32[48]{0:T(128)S(1)}, f32[48]{0:T(128)}, u32[]{:S(2)}) copy-start(f32[48]{0:T(128)} %param.31) | copy-start | bytes 580
  257.6 13.2 %copy-start.18 = (f32[48]{0:T(128)S(1)}, f32[48]{0:T(128)}, u32[]{:S(2)}) copy-start(f32[48]{0:T(128)} %param.43) | copy-start | bytes 580
  257.6 13.2 %copy-start.19 = (f32[48]{0:T(128)S(1)}, f32[48]{0:T(128)}, u32[]{:S(2)}) copy-start(f32[48]{0:T(128)} %param.39) | copy-start | bytes 580
  257.6 13.2 %copy-start.20 = (f32[48]{0:T(128)S(1)}, f32[48]{0:T(128)}, u32[]{:S(2)}) copy-start(f32[48]{0:T(128)} %param.35) | copy-start | bytes 580
  257.7 13.8 %copy-start.9 = (f32[8,384]{1,0:T(8,128)S(1)}, f32[8,384]{1,0:T(8,128)}, u32[]{:S(2)}) copy-start(f32[8,384]{1,0:T(8,128)} %vec.5) | copy-start | bytes 36868
  257.7 13.8 %copy-start.13 = (f32[8,384]{1,0:T(8,128)S(1)}, f32[8,384]{1,0:T(8,128)}, u32[]{:S(2)}) copy-start(f32[8,384]{1,0:T(8,128)} %param.44) | copy-start | bytes 36868
  257.7 13.8 %copy-start.14 = (f32[8,384]{1,0:T(8,128)S(1)}, f32[8,384]{1,0:T(8,128)}, u32[]{:S(2)}) copy-start(f32[8,384]{1,0:T(8,128)} %param.40) | copy-start | bytes 36868
  257.7 13.8 %copy-start.15 = (f32[8,384]{1,0:T(8,128)S(1)}, f32[8,384]{1,0:T(8,128)}, u32[]{:S(2)}) copy-start(f32[8,384]{1,0:T(8,128)} %param.36) | copy-start | bytes 36868
  257.7 52.0 %copy-start.2 = (f32[384,48]{0,1:T(8,128)S(1)}, f32[384,48]{0,1:T(8,128)}, u32[]{:S(2)}) copy-start(f32[384,48]{0,1:T(8,128)} %param.29) | copy-start | bytes 221188
  257.7 52.0 %copy-start.6 = (f32[384,48]{0,1:T(8,128)S(1)}, f32[384,48]{0,1:T(8,128)}, u32[]{:S(2)}) copy-start(f32[384,48]{0,1:T(8,128)} %param.41) | copy-start | bytes 221188
  257.7 52.0 %copy-start.7 = (f32[384,48]{0,1:T(8,128)S(1)}, f32[384,48]{0,1:T(8,128)}, u32[]{:S(2)}) copy-start(f32[384,48]{0,1:T(8,128)} %param.37) | copy-start | bytes 221188
  257.7 52.0 %copy-start.8 = (f32[384,48]{0,1:T(8,128)S(1)}, f32[384,48]{0,1:T(8,128)}, u32[]{:S(2)}) copy-start(f32[384,48]{0,1:T(8,128)} %param.33) | copy-start | bytes 221188
  257.8 155.2 %copy-start = (f32[2,384,48]{1,2,0:T(8,128)S(1)}, f32[2,384,48]{1,2,0:T(8,128)}, u32[]{:S(2)}) copy-start(f32[2,384,48]{1,2,0:T(8,128)} %param.30) | copy-start | bytes 442372
  257.8 155.2 %copy-start.3 = (f32[2,384,48]{1,2,0:T(8,128)S(1)}, f32[2,384,48]{1,2,0:T(8,128)}, u32[]{:S(2)}) copy-start(f32[2,384,48]{1,2,0:T(8,128)} %param.42) | copy-start | bytes 442372
  257.8 155.2 %copy-start.4 = (f32[2,384,48]{1,2,0:T(8,128)S(1)}, f32[2,384,48]{1,2,0:T(8,128)}, u32[]{:S(2)}) copy-start(f32[2,384,48]{1,2,0:T(8,128)} %param.38) | copy-start | bytes 442372
  257.8 155.2 %copy-start.5 = (f32[2,384,48]{1,2,0:T(8,128)S(1)}, f32[2,384,48]{1,2,0:T(8,128)}, u32[]{:S(2)}) copy-start(f32[2,384,48]{1,2,0:T(8,128)} %param.34) | copy-start | bytes 442372
  (1 other events, 0.8 us)
Sparse Core Ops, SparseCore 0:
  11.5 56.8 all-gather.2
  71.8 56.3 all-gather.4
  214.1 95.6 reduce-scatter.2
  314.9 98.0 reduce-scatter.4
